TPU v7x, 32 devices: a whole 2x2x4 slice. The times are simulated.
32 devices in a mesh: row: 8 (over y, x, core), col: 4 (over z).
Axes of the slice: x: 2, y: 2, z: 4, core: 2. Of those that a mesh axis runs over, the one named last changes fastest.
Arguments:
- density: bfloat16 [8192, 8192], P('col', 'row'), may hold values from -0.09375 to 0.09375
- hamiltonian: bfloat16 [8192, 8192], P('row', 'col'), may hold values from -6 to 6
- pattern_p: int32 [64, 64], P('col', 'row'), may hold values 0 or 1
- pattern_h: int32 [64, 64], P('row', 'col'), may hold values 0 or 1
- pattern_s: int32 [8, 64], P('col', 'row'), may hold values 0 or 1
- owner: int32 [4, 8, 16, 1], P('col', 'row'), may hold values from 0 to 3; in each aligned block of 16 rows (0 to 15, 16 to 31, ..., all dimensions but the last counted through in order) at most 8 rows name the same one
- d_intersection: bfloat16 [8, 4, 3, 32, 128, 128], P('row', 'col'), may hold values from -6 to 6
- d_hamilton: bfloat16 [8, 4, 3, 32, 128, 128], P('row', 'col'), may hold values from -6 to 6
Outputs:
- weighted: bfloat16 [1024, 8192], P('col', 'row')
- forces: float32 [8, 4, 3, 32], P('row', 'col')
Inputs may be any that keep to these rules, and one draw needn't show every extreme that they name: Among the 16 blocks of one device no owner is named more than 8 times.
All inputs are finite; a program needn't handle non-finite values. No bound on the sum of `pattern_p` or of `pattern_h` or of `pattern_s` on one device may be relied on, other than what follows from the above.
Results may differ from a plain program's by a relative error of at most 0.0049.
Values may be sent and summed in bfloat16 or wider, within the bound.
A program may use at most 128 MiB of HBM per device.

v0:
```python
import jax
import jax.numpy as jnp
from jax import lax
from jax.sharding import PartitionSpec as P

BLOCK = 128
CBLK = 8
SBLK = 2


def spread(matrix, pattern):
    rows, cols = matrix.shape
    rb, cb = pattern.shape
    tiles = matrix.reshape(rb, rows // rb, cb, cols // cb) * pattern[:, None, :, None].astype(
        matrix.dtype
    )
    return tiles.reshape(rows, cols)


def as_blocks(matrix):
    tiles = matrix.reshape(SBLK, BLOCK, CBLK, BLOCK).transpose(0, 2, 1, 3)
    return tiles.reshape(SBLK * CBLK, BLOCK * BLOCK)


def local(density, hamiltonian, pattern_p, pattern_h, pattern_s, owner, d_intersection, d_hamilton):
    masked_p = spread(density, pattern_p)
    masked_h = spread(hamiltonian, pattern_h)
    slab = masked_p[: SBLK * BLOCK]
    partial_value = jnp.dot(
        lax.all_gather(slab, "col", axis=0, tiled=True),
        masked_h,
        preferred_element_type=jnp.float32,
    )
    panel = lax.psum(partial_value, "row").astype(jnp.bfloat16)
    product = lax.psum_scatter(
        jnp.dot(panel, masked_p, preferred_element_type=jnp.float32),
        "col",
        scatter_dimension=0,
        tiled=True,
    )
    weighted = spread(product, pattern_s).astype(jnp.bfloat16)
    columns = lax.axis_size("col")
    slot_total = d_intersection.shape[3]
    capacity = slot_total // columns
    target = owner.reshape(SBLK * CBLK)
    onehot = (target[:, None] == jnp.arange(columns, dtype=jnp.int32)[None, :]).astype(jnp.int32)
    before = jnp.cumsum(onehot, axis=0) - onehot
    rank = jnp.sum(before * onehot, axis=1)
    slot_id = target * capacity + rank
    select = (jnp.arange(slot_total, dtype=jnp.int32)[:, None] == slot_id[None, :]).astype(
        jnp.bfloat16
    )
    blocks = jnp.concatenate((as_blocks(weighted), as_blocks(slab)), axis=1)
    outgoing = jnp.dot(select, blocks, preferred_element_type=jnp.float32).astype(jnp.bfloat16)
    width = BLOCK * BLOCK
    dov = d_intersection.reshape(3, slot_total, width)
    dham = d_hamilton.reshape(3, slot_total, width)
    sending = outgoing.reshape(columns, capacity, 2 * width)
    arrived = lax.all_to_all(sending, "col", split_axis=0, concat_axis=0, tiled=True).reshape(
        slot_total, 2, width
    )
    first = jnp.einsum("zsx,sx->zs", dham, arrived[:, 1], preferred_element_type=jnp.float32)
    second = jnp.einsum("zsx,sx->zs", dov, arrived[:, 0], preferred_element_type=jnp.float32)
    forces = (first - second) / BLOCK
    return (weighted, forces.reshape(1, 1, 3, slot_total))


def solution(mesh):
    in_specs = (
        P("col", "row"),
        P("row", "col"),
        P("col", "row"),
        P("row", "col"),
        P("col", "row"),
        P("col", "row", None, None),
        P("row", "col", None, None, None, None),
        P("row", "col", None, None, None, None),
    )
    out_specs = (P("col", "row"), P("row", "col", None, None))
    return jax.shard_map(local, mesh=mesh, in_specs=in_specs, out_specs=out_specs, check_vma=False)
```

profile of v0, /device:TPU:0, one launch (start us, length us, event | category | flops | bytes accessed | tf_op | source)
XLA Modules:
  0.0 411.4 jit_solution(1388677260380273171)
XLA Ops:
  7.2 0.7 convert_element_type.25
  8.0 3.3 copy.22
  11.3 1.9 copy-done
  13.3 0.9 copy.42
  14.3 48.7 %all-gather.2.cloned.1.call-done = bf16[1024,1024]{1,0:T(8,128)(2,1)} async-done(((bf16[256,1024]{1,0:T(8,128)(2,1)}), bf16[1024,1024]{1,0:T(8,128)(2,1)}) %all-gather.2.cloned.1.call-update) | async-done | bytes 2097168 | tf_op jit(solution)/shard_map/all_gather | solution.py:30
  63.1 0.6 mul.47
  63.7 1.6 copy-done.7
  65.2 8.8 %fusion.3 = f32[1024,2048]{1,0:T(8,128)} fusion(bf16[1024,1024]{1,0:T(8,128)(2,1)} %all-gather.2.cloned.1.call-done, bf16[1024,2048]{1,0:T(8,128)(2,1)S(1)} %copy-done.7, bf16[128,8,16,128]{3,2,1,0:T(8,128)(2,1)S(1)} %bitcast.69), kind=kOutput, calls=%fused_computation.6 | convolution fusion | flops 4297064448 | bytes 18874368 | tf_op jit(solution)/shard_map/dot_general | solution.py:29
  74.1 168.6 %all-reduce.1 = bf16[1024,2048]{1,0:T(8,128)(2,1)} all-reduce(f32[1024,2048]{1,0:T(8,128)} %fusion.3), channel_id=1, replica_groups=mesh['row'=8,'col'=4] {'row'}, use_global_device_ids=true, to_apply=%region_0.0 | all-reduce | flops 2097152 | bytes 12582912 | tf_op jit(solution)/shard_map/psum | solution.py:34
  243.3 1.6 copy-done.1
  244.9 8.3 %fusion.1 = f32[1024,1024]{1,0:T(8,128)} fusion(bf16[2048,1024]{1,0:T(8,128)(2,1)} %param.8, bf16[256,8,8,128]{3,2,1,0:T(8,128)(2,1)S(1)} %bitcast.67, bf16[1024,2048]{1,0:T(8,128)(2,1)S(1)} %copy-done.1), kind=kOutput, calls=%fused_computation.3 | convolution fusion | flops 4297064448 | bytes 16777216 | tf_op jit(solution)/shard_map/dot_general | solution.py:36
  253.1 0.7 copy-done.6
  254.1 1.2 fusion.21
  255.3 72.5 %reduce-scatter.2.cloned.1.call-done = f32[256,1024]{1,0:T(8,128)} async-done(((f32[1024,1024]{1,0:T(8,128)}), f32[256,1024]{1,0:T(8,128)}) %reduce-scatter.2.cloned.1.call-update) | async-done | bytes 1048592 | tf_op jit(solution)/shard_map/reduce_scatter | solution.py:35
  327.9 1.4 fusion.10
  329.3 0.8 copy-done.3
  330.2 2.0 fusion
  332.3 4.2 %all-to-all-start = ((bf16[4,8,32768]{2,1,0:T(8,128)(2,1)}), bf16[4,8,32768]{2,1,0:T(8,128)(2,1)S(1)}, u32[]{:S(2)}, u32[]{:S(2)}) async-start(bf16[4,8,32768]{2,1,0:T(8,128)(2,1)} %fusion), calls=%async_computation.1 | async-start | bytes 4194304 | tf_op jit(solution)/shard_map/all_to_all | solution.py:59
  336.5 5.8 %reshape.67 = bf16[3,32,16384]{2,1,0:T(8,128)(2,1)} reshape(bf16[1,1,3,32,128,128]{5,4,3,2,1,0:T(8,128)(2,1)} %param.15) | data formatting | bytes 6291456 | tf_op jit(solution)/shard_map/reshape | solution.py:57
  342.3 5.8 %reshape.68 = bf16[3,32,16384]{2,1,0:T(8,128)(2,1)} reshape(bf16[1,1,3,32,128,128]{5,4,3,2,1,0:T(8,128)(2,1)} %param.14) | data formatting | bytes 6291456 | tf_op jit(solution)/shard_map/reshape | solution.py:56
  348.1 36.8 %all-to-all-done = bf16[4,8,32768]{2,1,0:T(8,128)(2,1)S(1)} async-done(((bf16[4,8,32768]{2,1,0:T(8,128)(2,1)}), bf16[4,8,32768]{2,1,0:T(8,128)(2,1)S(1)}, u32[]{:S(2)}, u32[]{:S(2)}) %all-to-all-start) | async-done | bytes 2097184 | tf_op jit(solution)/shard_map/all_to_all | solution.py:59
  384.9 2.8 reshape.66
  387.7 8.8 %fusion.8 = f32[32,1,3]{2,1,0:T(1,128)S(1)} fusion(bf16[3,32,16384]{2,1,0:T(8,128)(2,1)} %reshape.67, bf16[32,2,16384]{2,1,0:T(2,128)(2,1)} %reshape.66), kind=kOutput, calls=%fused_computation.11 | convolution fusion | flops 3145728 | bytes 5243264 | tf_op jit(solution)/shard_map/zsx,sx->zs/dot_general | solution.py:62
  396.6 7.3 %fusion.6 = f32[32,1,3]{2,1,0:T(1,128)S(1)} fusion(bf16[3,32,16384]{2,1,0:T(8,128)(2,1)S(1)} %copy-done.2, bf16[32,2,16384]{2,1,0:T(2,128)(2,1)} %reshape.66), kind=kOutput, calls=%fused_computation.9 | convolution fusion | flops 3145728 | bytes 5243264 | tf_op jit(solution)/shard_map/zsx,sx->zs/dot_general | solution.py:63
  (32 shorter events, 2.3 us)
Async XLA Ops:
  7.2 55.9 %all-gather.2.cloned.1.call-start = ((), (), s32[]{:S(2)}) async-start(), calls=%async_computation.2 | async-start | bytes 2621440 | tf_op jit(solution)/shard_map/all_gather | solution.py:30
  8.0 6.3 %copy-start.4 = (s32[8,16]{1,0:T(8,128)S(1)}, s32[8,16]{1,0:T(8,128)}, u32[]{:S(2)}) copy-start(s32[8,16]{1,0:T(8,128)} %param.11) | copy-start | bytes 1540
  11.3 1.9 copy-start
  14.3 313.5 %reduce-scatter.2.cloned.1.call-start = ((), (), s32[]{:S(2)}) async-start(), calls=%async_computation.3 | async-start | bytes 5242880 | tf_op jit(solution)/shard_map/reduce_scatter | solution.py:35
  63.1 2.2 copy-start.7
  242.7 2.2 copy-start.1
  253.1 0.7 copy-start.6
  253.1 0.7 copy-start.5
  329.3 0.8 copy-start.3
  332.3 52.6 %all-to-all-start = ((bf16[4,8,32768]{2,1,0:T(8,128)(2,1)}), bf16[4,8,32768]{2,1,0:T(8,128)(2,1)S(1)}, u32[]{:S(2)}, u32[]{:S(2)}) async-start(bf16[4,8,32768]{2,1,0:T(8,128)(2,1)} %fusion), calls=%async_computation.1 | async-start | bytes 4194304 | tf_op jit(solution)/shard_map/all_to_all | solution.py:59
  387.7 8.9 %copy-start.2 = (bf16[3,32,16384]{2,1,0:T(8,128)(2,1)S(1)}, bf16[3,32,16384]{2,1,0:T(8,128)(2,1)}, u32[]{:S(2)}) copy-start(bf16[3,32,16384]{2,1,0:T(8,128)(2,1)} %reshape.68) | copy-start | bytes 9437188
Sparse Core Ops, SparseCore 0:
  14.4 48.6 all-gather.1
  253.3 74.4 reduce-scatter.1
where the time goes:
time: 412 us; the launch traced here: 411 us
  blocking collectives  169 us (41%)
  waiting for transfers between devices  158 us (38%)
  matrix products  35.3 us (9%)
  local copies, waits for them, and re-layouts  27.4 us (7%)
  between operations  14.1 us (3%)
  starting transfers between devices  4.27 us (1%)
    psum x1, blocking collectives, local(): panel = lax.psum(partial_value, 'row').astype(jnp.bfloat16)  169 us
    reduce_scatter x1, waiting for transfers between devices, local(): lax.psum_scatter(jnp.dot(panel, masked_p, preferred_element_type=jnp.floa...  72.5 us
    all_gather x1, waiting for transfers between devices, local(): lax.all_gather(slab, 'col', axis=0, tiled=True)  48.7 us
    all_to_all x1, waiting for transfers between devices, local(): lax.all_to_all(sending, 'col', split_axis=0, concat_axis=0, tiled=True)  36.8 us
    unnamed x20, local copies, waits for them, and re-layouts  11.4 us
    dot_general x1, matrix products, local(): jnp.dot(lax.all_gather(slab, 'col', axis=0, tiled=True), masked_h, prefer...  8.85 us
    dot_general x1, matrix products, local(): jnp.einsum('zsx,sx->zs', dham, arrived[:, 1], preferred_element_type=jnp....  8.82 us
    dot_general x1, matrix products, local(): jnp.dot(panel, masked_p, preferred_element_type=jnp.float32)  8.26 us
  transfers between devices with their start and end apart: 3, of which 3 were waited for; matrix products, arithmetic and copies ran while one was open for 3% of the time, Pallas kernels for 0%

commit v1 on v0

v1 whole, which is shorter than its diff:
```python
import functools

import jax
import jax.numpy as jnp
from jax import lax
from jax.experimental import pallas as pl
from jax.experimental.pallas import tpu as pltpu
from jax.sharding import PartitionSpec as P

BLOCK = 128
CBLK = 8
SBLK = 2
ROWS = SBLK * BLOCK
NBLK = SBLK * CBLK
BF = jnp.bfloat16
F32 = jnp.float32
MESH = pl.DeviceIdType.MESH


def spread(matrix, pattern):
    rows, cols = matrix.shape
    rb, cb = pattern.shape
    tiles = matrix.reshape(rb, rows // rb, cb, cols // cb) * pattern[:, None, :, None].astype(
        matrix.dtype
    )
    return tiles.reshape(rows, cols)


def rows_at(start, size):
    return pl.ds(pl.multiple_of(start, 16), size)


def main_kernel(nr, nc, cap, ps_ref, idx_ref, p_ref, h_ref, w_out, wr_out, pr_out,
                slab, acc, sbuf, rbuf, ybuf, wown, wrecv, blkp, blkw, op, ow, ip, iw,
                sl_s, sl_r, rs_s, rs_r, ag_s, ag_r, w_s, w_r, p_s, p_r, q_s, q_r):
    r = lax.axis_index("row")
    c = lax.axis_index("col")
    steps = nr.bit_length() - 1
    half = h_ref.shape[1] // 2
    bits = list(range(steps))
    orders = [bits, bits[:1] + bits[2:] + bits[1:2]]
    bit = [lax.rem(r // (1 << b), 2) for b in bits]
    mate = [r + (1 - 2 * bit[b]) * (1 << b) for b in bits]
    peer = [lax.rem(c + d, nc) for d in range(nc)]

    barrier = pltpu.get_barrier_semaphore()
    for b in bits:
        pl.semaphore_signal(barrier, inc=1, device_id=(mate[b], c), device_id_type=MESH)
    for d in range(1, nc):
        pl.semaphore_signal(barrier, inc=1, device_id=(r, peer[d]), device_id_type=MESH)
    pl.semaphore_wait(barrier, steps + nc - 1)

    def remote(src, dst, s, t, where):
        return pltpu.make_async_remote_copy(
            src_ref=src, dst_ref=dst, send_sem=s, recv_sem=t, device_id=where,
            device_id_type=MESH)

    order = sorted(range(nc), key=lambda d: (min(d, nc - d), d))
    slab_copy = {}
    for d in order[1:]:
        cp = remote(p_ref.at[pl.ds(0, ROWS)], slab.at[nc - d], sl_s.at[nc - d],
                    sl_r.at[nc - d], (r, peer[d]))
        cp.start()
        slab_copy[nc - d] = cp

    def route(blk, out, inn, s, t):
        copies = []
        for d in list(range(1, nc)) + [0]:
            def pick(q, carry, d=d):
                got = blk[idx_ref[peer[d] * cap + q]]
                if d == 0:
                    inn[c * cap + q] = got
                else:
                    out[d * cap + q] = got
                return carry
            lax.fori_loop(0, cap, pick, 0)
            if d:
                cp = remote(out.at[pl.ds(d * cap, cap)], inn.at[pl.ds(c * cap, cap)],
                            s.at[d], t.at[d], (r, peer[d]))
                cp.start()
                copies.append(cp)
        return copies

    rel = []
    for s in range(2):
        at = [0]
        for k in range(1, steps):
            at.append(at[-1] + bit[orders[s][k]] * (ROWS >> (k + 1)))
        rel.append([None] + at)
    base = bit[0] * (ROWS // 2)
    rs = {}
    ag = {}
    wc = {}

    def region(k):
        return pl.ds(ROWS - (ROWS >> k), ROWS >> (k + 1))

    def first(j):
        if j:
            slab_copy[j].wait()
        for send in (True, False):
            start = ROWS // 2 - base if send else base
            for s in range(2):
                def tile(t, carry, s=s, send=send, start=start):
                    cols = pl.ds(pl.multiple_of(t * 256, 256), 256)
                    hcol = pl.ds(pl.multiple_of(s * half + t * 256, 256), 256)
                    rows = rows_at(start, ROWS // 2)
                    a = slab[j, rows, :] if j else p_ref[rows, :]
                    v = jnp.dot(a, h_ref[:, hcol], preferred_element_type=F32)
                    if send:
                        sbuf[j, s, pl.ds(0, ROWS // 2), cols] = v.astype(BF)
                    else:
                        acc[j, s, :, cols] = v
                    return carry
                lax.fori_loop(0, half // 256, tile, 0)
                if send:
                    start_rs(j, s, 0)

    def start_rs(j, s, k):
        cp = remote(sbuf.at[j, s, region(k)], rbuf.at[j, s, region(k)], rs_s.at[j, s, k],
                    rs_r.at[j, s, k], (mate[orders[s][k]], c))
        cp.start()
        rs[j, s, k] = cp

    def reduce(j, k):
        for s in range(2):
            rs[j, s, k - 1].wait()
            size = ROWS >> k
            came = ROWS - (ROWS >> (k - 1))
            at = rel[s][k]
            if k == steps:
                def last(i, carry, s=s, at=at):
                    x = acc[j, s, rows_at(at + i * 16, 16), :]
                    y = rbuf[j, s, pl.ds(pl.multiple_of(came + i * 16, 16), 16), :].astype(F32)
                    ybuf[j, s, rows_at(base + at + i * 16, 16), :] = (x + y).astype(BF)
                    return carry
                lax.fori_loop(0, size // 16, last, 0)
                start_ag(j, s, k - 1)
            else:
                h = size // 2
                away = (1 - bit[orders[s][k]]) * h
                keep = bit[orders[s][k]] * h
                for off, send in ((away, True), (keep, False)):
                    def add(i, carry, s=s, at=at, off=off, send=send):
                        rows = rows_at(at + off + i * 16, 16)
                        y = rbuf[j, s, rows_at(came + off + i * 16, 16), :].astype(F32)
                        v = acc[j, s, rows, :] + y
                        if send:
                            sbuf[j, s, rows_at(ROWS - (ROWS >> k) + i * 16, 16), :] = v.astype(BF)
                        else:
                            acc[j, s, rows, :] = v
                        return carry
                    lax.fori_loop(0, h // 16, add, 0)
                    if send:
                        start_rs(j, s, k)

    def start_ag(j, s, k):
        seg = rows_at(base + rel[s][k + 1], ROWS >> (k + 1))
        cp = remote(ybuf.at[j, s, seg], ybuf.at[j, s, seg], ag_s.at[j, s, k], ag_r.at[j, s, k],
                    (mate[orders[s][k]], c))
        cp.start()
        ag[j, s, k] = cp

    def gather(j, k):
        for s in range(2):
            ag[j, s, k].wait()
            start_ag(j, s, k - 1)

    def second(j):
        for s in range(2):
            ag[j, s, 0].wait()

        def tile(t, carry):
            cols = pl.ds(pl.multiple_of(t * 256, 256), 256)
            v = jnp.dot(ybuf[j, 0], p_ref[pl.ds(0, half), cols], preferred_element_type=F32)
            v = v + jnp.dot(ybuf[j, 1], p_ref[pl.ds(half, half), cols],
                            preferred_element_type=F32)
            if j:
                sbuf[j, 0, :, cols] = v.astype(BF)
            else:
                wown[:, cols] = v
            return carry
        lax.fori_loop(0, CBLK * BLOCK // 256, tile, 0)
        if j:
            cp = remote(sbuf.at[j, 0], wrecv.at[j], w_s.at[j], w_r.at[j], (r, peer[j]))
            cp.start()
            wc[j] = cp

    stages = [first]
    stages += [functools.partial(lambda j, k: reduce(j, k), k=k) for k in range(1, steps + 1)]
    stages += [functools.partial(lambda j, k: gather(j, k), k=k) for k in range(steps - 1, 0, -1)]
    stages += [second]
    pcopies = []
    for t in range(nc + len(stages) - 1):
        for i in range(nc):
            if 0 <= t - i < len(stages):
                stages[t - i](order[i])
        if t == 0:
            for u in range(SBLK):
                for v in range(CBLK):
                    blkp[u * CBLK + v] = p_ref[pl.ds(u * BLOCK, BLOCK), pl.ds(v * BLOCK, BLOCK)]
            blkp[NBLK] = jnp.zeros((BLOCK, BLOCK), BF)
            blkw[NBLK] = jnp.zeros((BLOCK, BLOCK), BF)
        if t == nc - 1:
            pcopies = route(blkp, op, ip, p_s, p_r)

    for d in order[1:]:
        wc[d].wait()
    for u in range(SBLK):
        for v in range(CBLK):
            rows, cols = pl.ds(u * BLOCK, BLOCK), pl.ds(v * BLOCK, BLOCK)
            x = wown[rows, cols]
            for d in range(1, nc):
                x = x + wrecv[d, rows, cols].astype(F32)
            blkw[u * CBLK + v] = (x * ps_ref[u, v].astype(F32)).astype(BF)
    wcopies = route(blkw, ow, iw, q_s, q_r)
    for u in range(SBLK):
        for v in range(CBLK):
            w_out[pl.ds(u * BLOCK, BLOCK), pl.ds(v * BLOCK, BLOCK)] = blkw[u * CBLK + v]
    for cp in pcopies:
        cp.wait()

    def copy_p(i, carry):
        pr_out[i] = ip[i]
        return carry
    lax.fori_loop(0, nc * cap, copy_p, 0)
    for cp in wcopies:
        cp.wait()

    def copy_w(i, carry):
        wr_out[i] = iw[i]
        return carry
    lax.fori_loop(0, nc * cap, copy_w, 0)


def force_kernel(dh_ref, ds_ref, pr_ref, wr_ref, out_ref):
    for q in range(dh_ref.shape[1]):
        p = pr_ref[q].astype(F32)
        w = wr_ref[q].astype(F32)
        for z in range(3):
            t = dh_ref[z, q].astype(F32) * p - ds_ref[z, q].astype(F32) * w
            out_ref[z, q:q + 1, :] = jnp.sum(t, axis=0, keepdims=True)


def local(nr, nc, density, hamiltonian, pattern_p, pattern_h, pattern_s, owner, d_intersection,
          d_hamilton):
    masked_p = spread(density, pattern_p)
    masked_h = spread(hamiltonian, pattern_h)
    slots = d_intersection.shape[3]
    cap = slots // nc
    steps = nr.bit_length() - 1
    target = owner.reshape(NBLK)
    same = target[:, None] == target[None, :]
    number = jnp.arange(NBLK, dtype=jnp.int32)
    rank = jnp.sum(jnp.where(same & (number[None, :] < number[:, None]), 1, 0), axis=1)
    hit = jnp.arange(slots, dtype=jnp.int32)[:, None] == (target * cap + rank)[None, :]
    index = NBLK + jnp.sum(jnp.where(hit, number[None, :] - NBLK, 0), axis=1)
    half = hamiltonian.shape[1] // 2
    width = CBLK * BLOCK
    sem = pltpu.SemaphoreType.DMA
    smem = pl.BlockSpec(memory_space=pltpu.SMEM)
    vmem = pl.BlockSpec(memory_space=pltpu.VMEM)
    block = (BLOCK, BLOCK)
    weighted, wr, pr = pl.pallas_call(
        functools.partial(main_kernel, nr, nc, cap),
        out_shape=(jax.ShapeDtypeStruct((ROWS, width), BF),
                   jax.ShapeDtypeStruct((slots,) + block, BF),
                   jax.ShapeDtypeStruct((slots,) + block, BF)),
        in_specs=[smem, smem, vmem, vmem],
        out_specs=(vmem, vmem, vmem),
        scratch_shapes=[
            pltpu.VMEM((nc, ROWS, width), BF),
            pltpu.VMEM((nc, 2, ROWS // 2, half), F32),
            pltpu.VMEM((nc, 2, ROWS, half), BF),
            pltpu.VMEM((nc, 2, ROWS, half), BF),
            pltpu.VMEM((nc, 2, ROWS, half), BF),
            pltpu.VMEM((ROWS, width), F32),
            pltpu.VMEM((nc, ROWS, width), BF),
            pltpu.VMEM((NBLK + 1,) + block, BF),
            pltpu.VMEM((NBLK + 1,) + block, BF),
            pltpu.VMEM((slots,) + block, BF),
            pltpu.VMEM((slots,) + block, BF),
            pltpu.VMEM((slots,) + block, BF),
            pltpu.VMEM((slots,) + block, BF),
            sem((nc,)), sem((nc,)),
            sem((nc, 2, steps)), sem((nc, 2, steps)),
            sem((nc, 2, steps)), sem((nc, 2, steps)),
            sem((nc,)), sem((nc,)), sem((nc,)), sem((nc,)), sem((nc,)), sem((nc,)),
        ],
        compiler_params=pltpu.CompilerParams(
            collective_id=0, has_side_effects=True, vmem_limit_bytes=63 * 2**20),
        name="density_product",
    )(pattern_s, index, masked_p, masked_h)
    group = 8
    sums = pl.pallas_call(
        force_kernel,
        grid=(slots // group,),
        out_shape=jax.ShapeDtypeStruct((3, slots, BLOCK), F32),
        in_specs=[pl.BlockSpec((3, group) + block, lambda i: (0, i, 0, 0)),
                  pl.BlockSpec((3, group) + block, lambda i: (0, i, 0, 0)),
                  pl.BlockSpec((group,) + block, lambda i: (i, 0, 0)),
                  pl.BlockSpec((group,) + block, lambda i: (i, 0, 0))],
        out_specs=pl.BlockSpec((3, group, BLOCK), lambda i: (0, i, 0)),
        name="pair_forces",
    )(d_hamilton.reshape((3, slots) + block), d_intersection.reshape((3, slots) + block), pr, wr)
    forces = jnp.sum(sums, axis=-1) / BLOCK
    return (weighted, forces.reshape(1, 1, 3, slots))


def solution(mesh):
    nr, nc = mesh.shape["row"], mesh.shape["col"]
    in_specs = (
        P("col", "row"),
        P("row", "col"),
        P("col", "row"),
        P("row", "col"),
        P("col", "row"),
        P("col", "row", None, None),
        P("row", "col", None, None, None, None),
        P("row", "col", None, None, None, None),
    )
    out_specs = (P("col", "row"), P("row", "col", None, None))
    return jax.shard_map(functools.partial(local, nr, nc), mesh=mesh, in_specs=in_specs,
                         out_specs=out_specs, check_vma=False)
```

time: 412 us -> 170 us (0.41)
  blocking collectives: 169 us -> 0 us
  waiting for transfers between devices: 158 us -> 0 us
  Pallas kernels: 0 us -> 152 us
  matrix products: 35.3 us -> 0 us
  local copies, waits for them, and re-layouts: 27.4 us -> 4.98 us
  between operations: 14.1 us -> 0.68 us
  other arithmetic: 3.7 us -> 9.96 us
  starting transfers between devices: 4.27 us -> 0 us
    psum x1 -> x0, blocking collectives: 169 us -> none  [local(): panel = lax.psum(partial_value, 'row').astype(jnp.bfloat16)]
    pallas_call x0 -> x2, Pallas kernels: none -> 152 us  [the longest x1 147 us: local(): pl.pallas_call(functools.partial(main_kernel, nr, nc, cap), out_shape=(ja...]
    reduce_scatter x1 -> x0, waiting for transfers between devices: 72.5 us -> none  [local(): lax.psum_scatter(jnp.dot(panel, masked_p, preferred_element_type=jnp.floa...]
    all_gather x1 -> x0, waiting for transfers between devices: 48.7 us -> none  [local(): lax.all_gather(slab, 'col', axis=0, tiled=True)]
    all_to_all x1 -> x0, waiting for transfers between devices: 36.8 us -> none  [local(): lax.all_to_all(sending, 'col', split_axis=0, concat_axis=0, tiled=True)]
    dot_general x5 -> x0, matrix products: 35.3 us -> none  [the longest x1 8.85 us: local(): jnp.dot(lax.all_gather(slab, 'col', axis=0, tiled=True), masked_h, prefer...]
    reshape x4 -> x0, local copies, waits for them, and re-layouts: 14.5 us -> none  [the longest x1 5.81 us: local(): dham = d_hamilton.reshape(3, slot_total, width)]
    unnamed x20 -> x8, local copies, waits for them, and re-layouts: 11.4 us -> 3.69 us
  transfers between devices with their start and end apart: 3 -> 0, of which waited for: 3 -> 0; matrix products, arithmetic and copies ran while one was open for 3% -> 0% of each run, Pallas kernels for 0% -> 0%
where the time goes in v1:
time: 170 us; the launch traced here: 168 us
  Pallas kernels  152 us (89%)
  other arithmetic  9.96 us (6%)
  local copies, waits for them, and re-layouts  4.98 us (3%)
    pallas_call x1, Pallas kernels, local(): pl.pallas_call(functools.partial(main_kernel, nr, nc, cap), out_shape=(ja...  147 us
    mul x2, other arithmetic, spread(): matrix.reshape(rb, rows // rb, cb, cols // cb)  5.36 us
    pallas_call x1, Pallas kernels, local(): pl.pallas_call(force_kernel, grid=(slots // group,), out_shape=jax.ShapeD...  5.21 us
    unnamed x8, local copies, waits for them, and re-layouts  3.69 us

profile of v1, /device:TPU:0, one launch (start us, length us, event | category | flops | bytes accessed | tf_op | source)
XLA Modules:
  0.0 167.9 jit_solution(10933778338970773680)
XLA Ops:
  0.6 0.9 select_reduce_fusion.1
  1.5 0.7 iota_add_fusion
  2.2 0.1 select_reduce_fusion
  2.3 0.5 broadcast_add_fusion.idx_ref
  2.8 0.7 convert_element_type.8
  3.5 0.1 copy.12
  3.6 0.0 copy-start
  3.6 0.8 convert_element_type.9
  4.4 0.6 mul.30
  5.0 0.7 copy-done
  5.8 2.5 %bitcast_multiply_fusion.1.p_ref = bf16[2048,1024]{1,0:T(8,128)(2,1)} fusion(bf16[2048,1024]{1,0:T(8,128)(2,1)S(1)} %copy-done, bf16[256,8,8,128]{3,2,1,0:T(8,128)(2,1)S(1)} %bitcast.14), kind=kLoop, calls=%fused_computation.1 | loop fusion | flops 2097152 | bytes 12582912 | tf_op jit(solution)/shard_map/mul | solution.py:23
  8.3 0.0 copy-start.1
  8.3 0.6 mul.33
  8.9 1.6 copy-done.1
  10.4 2.9 %bitcast_multiply_fusion.h_ref = bf16[1024,2048]{1,0:T(8,128)(2,1)} fusion(bf16[1024,2048]{1,0:T(8,128)(2,1)S(1)} %copy-done.1, bf16[128,8,16,128]{3,2,1,0:T(8,128)(2,1)S(1)} %bitcast.15), kind=kLoop, calls=%fused_computation | loop fusion | flops 2097152 | bytes 12582912 | tf_op jit(solution)/shard_map/mul | solution.py:23
  13.3 147.0 %density_product.1 = (bf16[256,1024]{1,0:T(8,128)(2,1)}, bf16[32,128,128]{2,1,0:T(8,128)(2,1)}, bf16[32,128,128]{2,1,0:T(8,128)(2,1)}) custom-call(s32[2,8]{1,0:T(2,128)} %ps_ref.1, s32[32]{0:T(128)} %broadcast_add_fusion.idx_ref, bf16[2048,1024]{1,0:T(8,128)(2,1)} %bitcast_multiply_fusion.1.p_ref, bf16[1024,2048]{1,0:T(8,128)(2,1)} %bitcast_multiply_fusion.h_ref), custom_call_target="tpu_custom_call" | custom-call | tf_op jit(solution)/shard_map/density_product/pallas_call | solution.py:264
  160.4 0.0 copy-start.2
  160.4 5.2 %pair_forces.1 = f32[3,32,128]{2,1,0:T(8,128)} custom-call(bf16[3,32,128,128]{3,2,1,0:T(8,128)(2,1)} %bitcast.16, bf16[3,32,128,128]{3,2,1,0:T(8,128)(2,1)} %bitcast.17, bf16[32,128,128]{2,1,0:T(8,128)(2,1)} %get-tuple-element.6.pr_ref, bf16[32,128,128]{2,1,0:T(8,128)(2,1)} %get-tuple-element.7.wr_ref), custom_call_target="tpu_custom_call" | custom-call | tf_op jit(solution)/shard_map/pair_forces/pallas_call | solution.py:295
  165.6 0.9 reduce_sum.29
  166.5 0.6 copy.13
  167.1 0.0 copy-done.2
  167.1 0.8 copy.19
  (1 shorter events, 0.0 us)
Async XLA Ops:
  3.6 2.2 %copy-start = (bf16[2048,1024]{1,0:T(8,128)(2,1)S(1)}, bf16[2048,1024]{1,0:T(8,128)(2,1)}, u32[]{:S(2)}) copy-start(bf16[2048,1024]{1,0:T(8,128)(2,1)} %param.8) | copy-start | bytes 12582916
  8.3 2.2 %copy-start.1 = (bf16[1024,2048]{1,0:T(8,128)(2,1)S(1)}, bf16[1024,2048]{1,0:T(8,128)(2,1)}, u32[]{:S(2)}) copy-start(bf16[1024,2048]{1,0:T(8,128)(2,1)} %param.9) | copy-start | bytes 12582916
  160.4 6.7 %copy-start.2 = (bf16[256,1024]{1,0:T(8,128)(2,1)S(1)}, bf16[256,1024]{1,0:T(8,128)(2,1)}, u32[]{:S(2)}) copy-start(bf16[256,1024]{1,0:T(8,128)(2,1)} %get-tuple-element.16) | copy-start | bytes 1572868

commit v2 on v1

--- a/solution.py
+++ b/solution.py
@@ -17,21 +17,12 @@
 MESH = pl.DeviceIdType.MESH
 
 
-def spread(matrix, pattern):
-    rows, cols = matrix.shape
-    rb, cb = pattern.shape
-    tiles = matrix.reshape(rb, rows // rb, cb, cols // cb) * pattern[:, None, :, None].astype(
-        matrix.dtype
-    )
-    return tiles.reshape(rows, cols)
-
-
 def rows_at(start, size):
     return pl.ds(pl.multiple_of(start, 16), size)
 
 
-def main_kernel(nr, nc, cap, ps_ref, idx_ref, p_ref, h_ref, w_out, wr_out, pr_out,
-                slab, acc, sbuf, rbuf, ybuf, wown, wrecv, blkp, blkw, op, ow, ip, iw,
+def main_kernel(nr, nc, cap, ps_ref, idx_ref, pp_ref, ph_ref, p_hbm, h_hbm, w_out, wr_out,
+                pr_out, p_ref, h_ref, ld, slab, acc, sbuf, rbuf, ybuf, wown, wrecv, blkp, blkw, op, ow, ip, iw,
                 sl_s, sl_r, rs_s, rs_r, ag_s, ag_r, w_s, w_r, p_s, p_r, q_s, q_r):
     r = lax.axis_index("row")
     c = lax.axis_index("col")
@@ -43,6 +34,37 @@
     mate = [r + (1 - 2 * bit[b]) * (1 << b) for b in bits]
     peer = [lax.rem(c + d, nc) for d in range(nc)]
 
+    depth = p_ref.shape[0]
+    loads = [
+        pltpu.make_async_copy(p_hbm.at[pl.ds(0, ROWS)], p_ref.at[pl.ds(0, ROWS)], ld.at[0]),
+        pltpu.make_async_copy(h_hbm, h_ref, ld.at[1]),
+        pltpu.make_async_copy(p_hbm.at[pl.ds(ROWS, depth - ROWS)],
+                              p_ref.at[pl.ds(ROWS, depth - ROWS)], ld.at[2]),
+    ]
+    for load in loads:
+        load.start()
+
+    def mask(ref, pattern, low, high):
+        def line(a, carry):
+            rows = pl.ds(pl.multiple_of(a * BLOCK, BLOCK), BLOCK)
+            for b in range(ref.shape[1] // BLOCK):
+                cols = pl.ds(b * BLOCK, BLOCK)
+                ref[rows, cols] = (ref[rows, cols].astype(F32)
+                                   * pattern[a, b].astype(F32)).astype(BF)
+            return carry
+        lax.fori_loop(low, high, line, 0)
+
+    left = (nc - 1 - 2 * c + nc) // nc
+    near = left * c + (1 - left) * (nc - 1 - c)
+    jd = [0]
+    for i in range(1, nc):
+        far = (i - 2 * near - 1 + nc) // nc
+        ahead = (i + 1) // 2 if i % 2 else nc - i // 2
+        d = i - near
+        jd.append(far * (left * d + (1 - left) * (nc - d)) + (1 - far) * ahead)
+
+    loads[0].wait()
+    mask(p_ref, pp_ref, 0, SBLK)
     barrier = pltpu.get_barrier_semaphore()
     for b in bits:
         pl.semaphore_signal(barrier, inc=1, device_id=(mate[b], c), device_id_type=MESH)
@@ -55,13 +77,22 @@
             src_ref=src, dst_ref=dst, send_sem=s, recv_sem=t, device_id=where,
             device_id_type=MESH)
 
-    order = sorted(range(nc), key=lambda d: (min(d, nc - d), d))
-    slab_copy = {}
-    for d in order[1:]:
-        cp = remote(p_ref.at[pl.ds(0, ROWS)], slab.at[nc - d], sl_s.at[nc - d],
-                    sl_r.at[nc - d], (r, peer[d]))
-        cp.start()
-        slab_copy[nc - d] = cp
+    own = p_ref.at[pl.ds(0, ROWS)]
+    to_right = remote(own, slab.at[nc - 1], sl_s.at[0], sl_r.at[nc - 1], (r, c + 1))
+    to_left = remote(own, slab.at[1], sl_s.at[nc], sl_r.at[1], (r, c - 1))
+    sent = [(c + 1 < nc, to_right), (c > 0, to_left)]
+    for there, cp in sent:
+        pl.when(there)(cp.start)
+
+    def arrive(i):
+        j = jd[i]
+        step = 2 * ((c + j) // nc) - 1
+        cp = remote(slab.at[j], slab.at[j - step], sl_s.at[i], sl_r.at[j - step], (r, c + step))
+        come = remote(own, slab.at[j], sl_s.at[i], sl_r.at[j], (r, peer[1]))
+        come.wait_recv()
+        there = (c + step >= 0) & (c + step < nc)
+        pl.when(there)(cp.start)
+        sent.append((there, cp))
 
     def route(blk, out, inn, s, t):
         copies = []
@@ -97,7 +128,7 @@
 
     def first(j):
         if j:
-            slab_copy[j].wait()
+            arrive(j)
         for send in (True, False):
             start = ROWS // 2 - base if send else base
             for s in range(2):
@@ -105,7 +136,7 @@
                     cols = pl.ds(pl.multiple_of(t * 256, 256), 256)
                     hcol = pl.ds(pl.multiple_of(s * half + t * 256, 256), 256)
                     rows = rows_at(start, ROWS // 2)
-                    a = slab[j, rows, :] if j else p_ref[rows, :]
+                    a = slab[jd[j], rows, :] if j else p_ref[rows, :]
                     v = jnp.dot(a, h_ref[:, hcol], preferred_element_type=F32)
                     if send:
                         sbuf[j, s, pl.ds(0, ROWS // 2), cols] = v.astype(BF)
@@ -182,7 +213,8 @@
             return carry
         lax.fori_loop(0, CBLK * BLOCK // 256, tile, 0)
         if j:
-            cp = remote(sbuf.at[j, 0], wrecv.at[j], w_s.at[j], w_r.at[j], (r, peer[j]))
+            cp = remote(sbuf.at[j, 0], wrecv.at[jd[j]], w_s.at[j], w_r.at[jd[j]],
+                        (r, lax.rem(c + jd[j], nc)))
             cp.start()
             wc[j] = cp
 
@@ -191,11 +223,15 @@
     stages += [functools.partial(lambda j, k: gather(j, k), k=k) for k in range(steps - 1, 0, -1)]
     stages += [second]
     pcopies = []
+    loads[1].wait()
+    mask(h_ref, ph_ref, 0, h_ref.shape[0] // BLOCK)
     for t in range(nc + len(stages) - 1):
         for i in range(nc):
             if 0 <= t - i < len(stages):
-                stages[t - i](order[i])
+                stages[t - i](i)
         if t == 0:
+            loads[2].wait()
+            mask(p_ref, pp_ref, SBLK, depth // BLOCK)
             for u in range(SBLK):
                 for v in range(CBLK):
                     blkp[u * CBLK + v] = p_ref[pl.ds(u * BLOCK, BLOCK), pl.ds(v * BLOCK, BLOCK)]
@@ -204,7 +240,9 @@
         if t == nc - 1:
             pcopies = route(blkp, op, ip, p_s, p_r)
 
-    for d in order[1:]:
+    for there, cp in sent:
+        pl.when(there)(cp.wait_send)
+    for d in range(1, nc):
         wc[d].wait()
     for u in range(SBLK):
         for v in range(CBLK):
@@ -244,8 +282,6 @@
 
 def local(nr, nc, density, hamiltonian, pattern_p, pattern_h, pattern_s, owner, d_intersection,
           d_hamilton):
-    masked_p = spread(density, pattern_p)
-    masked_h = spread(hamiltonian, pattern_h)
     slots = d_intersection.shape[3]
     cap = slots // nc
     steps = nr.bit_length() - 1
@@ -266,9 +302,10 @@
         out_shape=(jax.ShapeDtypeStruct((ROWS, width), BF),
                    jax.ShapeDtypeStruct((slots,) + block, BF),
                    jax.ShapeDtypeStruct((slots,) + block, BF)),
-        in_specs=[smem, smem, vmem, vmem],
+        in_specs=[smem] * 4 + [pl.BlockSpec(memory_space=pl.ANY)] * 2,
         out_specs=(vmem, vmem, vmem),
         scratch_shapes=[
+            pltpu.VMEM(density.shape, BF), pltpu.VMEM(hamiltonian.shape, BF), sem((3,)),
             pltpu.VMEM((nc, ROWS, width), BF),
             pltpu.VMEM((nc, 2, ROWS // 2, half), F32),
             pltpu.VMEM((nc, 2, ROWS, half), BF),
@@ -282,7 +319,7 @@
             pltpu.VMEM((slots,) + block, BF),
             pltpu.VMEM((slots,) + block, BF),
             pltpu.VMEM((slots,) + block, BF),
-            sem((nc,)), sem((nc,)),
+            sem((nc + 1,)), sem((nc,)),
             sem((nc, 2, steps)), sem((nc, 2, steps)),
             sem((nc, 2, steps)), sem((nc, 2, steps)),
             sem((nc,)), sem((nc,)), sem((nc,)), sem((nc,)), sem((nc,)), sem((nc,)),
@@ -290,7 +327,7 @@
         compiler_params=pltpu.CompilerParams(
             collective_id=0, has_side_effects=True, vmem_limit_bytes=63 * 2**20),
         name="density_product",
-    )(pattern_s, index, masked_p, masked_h)
+    )(pattern_s, index, pattern_p, pattern_h, density, hamiltonian)
     group = 8
     sums = pl.pallas_call(
         force_kernel,

time: 170 us -> 160 us (0.941)
  other arithmetic: 9.96 us -> 3.07 us
  local copies, waits for them, and re-layouts: 4.98 us -> 2.72 us
    mul x2 -> x0, other arithmetic: 5.36 us -> none  [spread(): matrix.reshape(rb, rows // rb, cb, cols // cb)]
    unnamed x8 -> x5, local copies, waits for them, and re-layouts: 3.69 us -> 2.72 us
where the time goes in v2:
time: 160 us; the launch traced here: 159 us
  Pallas kernels  153 us (96%)
  other arithmetic  3.07 us (2%)
  local copies, waits for them, and re-layouts  2.72 us (2%)
    pallas_call x1, Pallas kernels, local(): pl.pallas_call(functools.partial(main_kernel, nr, nc, cap), out_shape=(ja...  148 us
    pallas_call x1, Pallas kernels, local(): pl.pallas_call(force_kernel, grid=(slots // group,), out_shape=jax.ShapeD...  5.21 us

profile of v2, /device:TPU:0, one launch (start us, length us, event | category | flops | bytes accessed | tf_op | source)
XLA Modules:
  0.0 159.4 jit_solution(15596876215712936799)
XLA Ops:
  0.6 0.9 select_reduce_fusion.1
  1.5 0.7 iota_add_fusion
  2.2 0.1 select_reduce_fusion
  2.3 0.5 broadcast_add_fusion.idx_ref
  2.8 1.4 copy.12.pp_ref
  4.2 147.7 %density_product.1 = (bf16[256,1024]{1,0:T(8,128)(2,1)}, bf16[32,128,128]{2,1,0:T(8,128)(2,1)}, bf16[32,128,128]{2,1,0:T(8,128)(2,1)}) custom-call(s32[2,8]{1,0:T(2,128)} %ps_ref.1, s32[32]{0:T(128)} %broadcast_add_fusion.idx_ref, s32[16,8]{1,0:T(8,128)} %copy.12.pp_ref, s32[8,16]{1,0:T(8,128)} %ph_ref.1, bf16[2048,1024]{1,0:T(8,128)(2,1)} %p_hbm.1, ...), custom_call_target="tpu_custom_call" | custom-call | tf_op jit(solution)/shard_map/density_product/pallas_call | solution.py:300
  151.9 0.0 copy-start
  151.9 5.2 %pair_forces.1 = f32[3,32,128]{2,1,0:T(8,128)} custom-call(bf16[3,32,128,128]{3,2,1,0:T(8,128)(2,1)} %bitcast.6, bf16[3,32,128,128]{3,2,1,0:T(8,128)(2,1)} %bitcast.7, bf16[32,128,128]{2,1,0:T(8,128)(2,1)} %get-tuple-element.6.pr_ref, bf16[32,128,128]{2,1,0:T(8,128)(2,1)} %get-tuple-element.7.wr_ref), custom_call_target="tpu_custom_call" | custom-call | tf_op jit(solution)/shard_map/pair_forces/pallas_call | solution.py:332
  157.1 0.9 reduce_sum.29
  158.0 0.6 copy.13
  158.6 0.0 copy-done
  158.6 0.8 copy.15
  (1 shorter events, 0.0 us)
Async XLA Ops:
  151.9 6.7 %copy-start = (bf16[256,1024]{1,0:T(8,128)(2,1)S(1)}, bf16[256,1024]{1,0:T(8,128)(2,1)}, u32[]{:S(2)}) copy-start(bf16[256,1024]{1,0:T(8,128)(2,1)} %get-tuple-element.16) | copy-start | bytes 1572868
